TPU v7x, 32 devices: a whole 2x2x4 slice. The times are simulated.
32 devices in a mesh: batch: 8 (over z, y), seq: 4 (over x, core).
Axes of the slice: x: 2, y: 2, z: 4, core: 2. Of those that a mesh axis runs over, the one named last changes fastest.
Arguments:
- layer_input: float32 [16, 512, 768], P('batch', 'seq'), may hold values from -6 to 6
- lengths: int32 [16], P('batch'), may hold values from 1 to 512, as said below
- attn_weight: float32 [4, 768, 768], P(None, 'batch')
- up_weight: float32 [768, 3072], P('batch'), may hold values from -0.21875 to 0.21875
- down_weight: float32 [3072, 768], P('batch'), may hold values from -0.109375 to 0.109375
- vectors: float32 [12, 768], P(None, 'batch')
- attn_moment: float32 [4, 768, 768], P(None, 'batch'), may hold values from -96 to 96
- up_moment: float32 [768, 3072], P('batch'), may hold values from -96 to 96
- down_moment: float32 [3072, 768], P('batch'), may hold values from -96 to 96
- vector_moment: float32 [12, 768], P(None, 'batch'), may hold values from -192 to 192
- out_grad: float32 [16, 512, 768], P('batch', 'seq'), may hold values from -6 to 6
- pool_grad: float32 [16, 768], P('batch', 'seq'), may hold values from -6 to 6
Outputs:
- layer_output: float32 [16, 512, 768], P('batch', 'seq')
- pooled: float32 [16, 768], P('batch', 'seq')
- input_grad: float32 [16, 512, 768], P('batch', 'seq')
- attn_grad: float32 [4, 768, 768], P(None, 'batch')
- up_grad: float32 [768, 3072], P('batch')
- down_grad: float32 [3072, 768], P('batch')
- vector_grad: float32 [12, 768], P(None, 'batch')
- attn_moment_new: float32 [4, 768, 768], P(None, 'batch')
- up_moment_new: float32 [768, 3072], P('batch')
- down_moment_new: float32 [3072, 768], P('batch')
- vector_moment_new: float32 [12, 768], P(None, 'batch')
- attn_new: float32 [4, 768, 768], P(None, 'batch')
- up_new: float32 [768, 3072], P('batch')
- down_new: float32 [3072, 768], P('batch')
- vectors_new: float32 [12, 768], P(None, 'batch')
Inputs may be any that keep to these rules, and one draw needn't show every extreme that they name: `lengths`: among the 2 aligned rows of each batch index one row has length 512.
All inputs are finite; a program needn't handle non-finite values.
Results may differ from a plain program's by a relative error of at most 0.015.
The roundings to bfloat16 on the way count: a program that leaves them out, or rounds other values in their place, can miss the bound.
Values may be sent and summed in bfloat16 or wider, within the bound.
A program may use at most 320 MiB of HBM per device.

v0:
```python
import math
import types

import jax
import jax.numpy as jnp
from jax import lax
from jax.experimental import pallas as pl
from jax.experimental.pallas import tpu as pltpu
from jax.sharding import PartitionSpec as P

H = 12
HD = 64
NS = 5
SEQ = 4
HEADS = H // SEQ

norm_eps = 1e-12
tiny_norm = 1e-07
matrix_decay = 0.95
vector_decay = 0.5
matrix_rate = 0.5
vector_rate = 0.03

MESH = pl.DeviceIdType.MESH
F32 = jnp.float32
BF16 = jnp.bfloat16


def coords(n):
    b = lax.axis_index("batch")
    s = lax.axis_index("seq")
    return b, s, b // 2, b % 2, n // 2


def remote(src, dst, send, recv, device):
    return pltpu.make_async_remote_copy(
        src_ref=src, dst_ref=dst, send_sem=send, recv_sem=recv, device_id=device, device_id_type=MESH
    )


class GatherBatch:
    peers = ("batch",)

    def __init__(self, n, src, eager=True):
        self.n = n
        self.eager = eager
        self.ins = [src]
        self.outs = [jax.ShapeDtypeStruct((n,) + src.shape, src.dtype)]
        m = n // 2
        self.scratch = [pltpu.SemaphoreType.DMA((2, m))] * 4 + [pltpu.SemaphoreType.DMA]

    def run(self, src, dst, zs, zr, ys, yr, own):
        b, s, hi, lo, m = coords(self.n)
        pair = (hi * 2 + 1 - lo, s)
        local = pltpu.make_async_copy(src, dst.at[b], own)
        local.start()

        def exists(way, d):
            return hi >= d if way == 0 else hi + d < m

        def ahead(way):
            return hi + 1 < m if way == 0 else hi >= 1

        def block_of(way, d):
            place = jnp.clip(hi - d if way == 0 else hi + d, 0, m - 1)
            return place * 2 + lo

        def along(way, d, ref):
            place = jnp.clip(hi + 1 if way == 0 else hi - 1, 0, m - 1)
            return remote(
                ref, dst.at[block_of(way, d)], zs.at[way, d], zr.at[way, d + 1], (place * 2 + lo, s)
            )

        def aside(way, d):
            place = dst.at[block_of(way, d)]
            return remote(place, place, ys.at[way, d], yr.at[way, d], pair)

        first = remote(src, dst.at[b], ys.at[0, 0], yr.at[0, 0], pair)
        for way in (0, 1):

            @pl.when(ahead(way))
            def _(way=way):
                along(way, 0, src).start()

        if not self.eager:
            yield
        first.start()
        yield
        for d in range(1, m):
            for way in (0, 1):

                @pl.when(exists(way, d))
                def _(way=way, d=d):
                    place = dst.at[block_of(way, d)]
                    remote(place, place, zs.at[way, d], zr.at[way, d], pair).wait_recv()
                    if d < m - 1:

                        @pl.when(ahead(way))
                        def _():
                            along(way, d, place).start()

                    aside(way, d).start()

            yield
        local.wait()
        first.wait()
        for d in range(m):
            for way in (0, 1):
                if d > 0:

                    @pl.when(exists(way, d))
                    def _(way=way, d=d):
                        aside(way, d).wait()

                if d < m - 1:

                    @pl.when(exists(way, d) & ahead(way))
                    def _(way=way, d=d):
                        along(way, d, dst.at[block_of(way, d)]).wait_send()


class GatherDirect:
    peers = ("all",)

    def __init__(self, n, src):
        self.n = n
        self.ins = [src]
        self.outs = [jax.ShapeDtypeStruct((n,) + src.shape, src.dtype)]
        self.scratch = [pltpu.SemaphoreType.DMA((n,))] * 2 + [pltpu.SemaphoreType.DMA]

    def run(self, src, dst, ss, rs, own):
        n = self.n
        b, s = lax.axis_index("batch"), lax.axis_index("seq")
        local = pltpu.make_async_copy(src, dst.at[b], own)
        local.start()
        copies = [
            remote(src, dst.at[b], ss.at[k], rs.at[k], ((b + k) % n, s)) for k in range(1, n)
        ]
        for c in copies:
            c.start()
        yield
        local.wait()
        for c in copies:
            c.wait()


class ScatterBatch:
    peers = ("batch",)

    def __init__(self, n, src, wire=BF16):
        self.n = n
        self.wire = wire
        self.ins = [src]
        shape = src.shape[1:]
        self.outs = [jax.ShapeDtypeStruct(shape, F32)]
        m = n // 2
        self.scratch = [pltpu.VMEM((m,) + shape, wire)] * 4 + [pltpu.SemaphoreType.DMA((m,))] * 4

    def run(self, src, dst, ysend, yrecv, zsend, zrecv, ys, yr, zs, zr):
        b, s, hi, lo, m = coords(self.n)
        pair = (hi * 2 + 1 - lo, s)
        first = {}
        order = list(range(1, m)) + [0]
        for d in order:
            h = (hi + d) % m
            ysend[d] = src[h * 2 + 1 - lo].astype(self.wire)
            first[d] = remote(ysend.at[d], yrecv.at[d], ys.at[d], yr.at[d], pair)
            first[d].start()
        yield
        second = []
        for d in range(1, m):
            h = (hi + d) % m
            first[d].wait_recv()
            zsend[d] = (src[h * 2 + lo] + yrecv[d].astype(F32)).astype(self.wire)
            c = remote(zsend.at[d], zrecv.at[d], zs.at[d], zr.at[d], (h * 2 + lo, s))
            c.start()
            second.append(c)
            yield
        first[0].wait_recv()
        total = src[b] + yrecv[0].astype(F32)
        for d in range(1, m):
            second[d - 1].wait_recv()
            total = total + zrecv[d].astype(F32)
        dst[...] = total
        for c in list(first.values()) + second:
            c.wait_send()


class GatherSeq:
    peers = ("seq",)

    def __init__(self, n, src):
        self.ins = [src]
        self.outs = [jax.ShapeDtypeStruct((SEQ,) + src.shape, src.dtype)]
        self.scratch = [pltpu.SemaphoreType.DMA((3,))] * 2 + [pltpu.SemaphoreType.DMA]

    def run(self, src, dst, ss, rs, own):
        b, s = lax.axis_index("batch"), lax.axis_index("seq")
        far, near = (s + 2) % 4, s + 1 - 2 * (s % 2)
        across = remote(src, dst.at[s], ss.at[0], rs.at[0], (b, far))
        across.start()
        local = pltpu.make_async_copy(src, dst.at[s], own)
        local.start()
        beside = remote(src, dst.at[s], ss.at[1], rs.at[1], (b, near))
        beside.start()
        yield
        across.wait_recv()
        passed = remote(dst.at[far], dst.at[far], ss.at[2], rs.at[2], (b, near))
        passed.start()
        yield
        local.wait()
        beside.wait()
        passed.wait()
        across.wait_send()


def owner_list(n):
    return [(0, 2), (1, 0), (n - 2, 2), (n - 1, 0), (n // 4, 0), (n // 2 + 1, 2)]


class OwnerMail:
    @staticmethod
    def scratch(n, count, relayed=None):
        dma = pltpu.SemaphoreType.DMA
        base = [dma((count,)), dma((SEQ * n,)), dma]
        if relayed is not None:
            base += [pltpu.VMEM((count, 2) + relayed, BF16), dma((count, 2)), dma((count, 2))]
        return base

    def __init__(self, n, places, inbox, ss, rs, own, relayed=None, relay_s=None, relay_r=None):
        self.n, self.places, self.inbox, self.ss, self.rs, self.own = n, places, inbox, ss, rs, own
        self.relayed, self.relay_s, self.relay_r = relayed, relay_s, relay_r
        self.b, self.s = lax.axis_index("batch"), lax.axis_index("seq")
        self.me = self.s * n + self.b
        self.mine = [(self.b == ob) & (self.s == os) for ob, os in places]

    def slot(self, seq, block):
        if len(self.inbox.shape) == 4:
            return self.inbox.at[seq, block]
        rows = self.inbox.shape[1] // self.n
        return self.inbox.at[seq, pl.ds(pl.multiple_of(block * rows, rows), rows)]

    def indirect(self, k):
        ob, os = self.places[k]
        hi, oh = self.b // 2, ob // 2
        light = hi < oh if oh < self.n // 4 else hi > oh
        same_lo, same_x = self.b % 2 == ob % 2, self.s // 2 == os // 2
        other_lo, other_x = jnp.logical_not(same_lo), jnp.logical_not(same_x)
        away = hi != oh
        column = away & same_lo & same_x
        return (away & other_lo & other_x, light & other_lo & same_x), (column, column & light)

    def copy(self, k, src):
        ob, os = self.places[k]
        place = self.slot(self.s, self.b)
        return remote(src, place, self.ss.at[k], self.rs.at[self.me], (ob, os))

    def aside(self, k, slot, src):
        across = self.b + 1 - 2 * (self.b % 2)
        seq = self.s if slot else (self.s + 2) % 4
        return remote(
            src, self.relayed.at[k, slot], self.ss.at[k], self.relay_r.at[k, slot], (across, seq)
        )

    def pass_copy(self, k, slot):
        block, seq = self.b + 1 - 2 * (self.b % 2), self.s if slot else (self.s + 2) % 4
        return remote(
            self.relayed.at[k, slot], self.slot(seq, block), self.relay_s.at[k, slot],
            self.rs.at[seq * self.n + block], self.places[k],
        )

    def send(self, k, src):
        direct = jnp.logical_not(self.mine[k])
        if self.relayed is not None:
            for slot, by_relay in enumerate(self.indirect(k)[0]):
                direct = direct & jnp.logical_not(by_relay)

                @pl.when(by_relay)
                def _(slot=slot):
                    self.aside(k, slot, src).start()

        @pl.when(direct)
        def _():
            self.copy(k, src).start()

        @pl.when(self.mine[k])
        def _():
            pltpu.make_async_copy(src, self.slot(self.s, self.b), self.own).start()

    def relay(self, k):
        for slot, here in enumerate(self.indirect(k)[1]):

            @pl.when(here)
            def _(slot=slot):
                place = self.relayed.at[k, slot]
                remote(
                    place, place, self.relay_s.at[k, slot], self.relay_r.at[k, slot], (0, 0)
                ).wait_recv()
                self.pass_copy(k, slot).start()

    def collect(self):
        place = self.slot(self.s, self.b)
        pltpu.make_async_copy(place, place, self.own).wait()

        @pl.loop(1, SEQ * self.n)
        def _(k):
            other = (self.me + k) % (SEQ * self.n)
            place = self.slot(other // self.n, other % self.n)
            remote(place, place, self.ss.at[0], self.rs.at[other], (0, 0)).wait_recv()

    def finish(self, k, src):
        @pl.when(jnp.logical_not(self.mine[k]))
        def _():
            self.copy(k, src).wait_send()

        if self.relayed is not None:

            for slot, here in enumerate(self.indirect(k)[1]):

                @pl.when(here)
                def _(slot=slot):
                    self.pass_copy(k, slot).wait_send()


class Muon:
    peers = ("all",)

    def __init__(self, n, attn_piece, wide_piece=None, wide_in=None):
        self.n = n
        self.ready = wide_in is not None
        self.ins = [attn_piece, wide_in if self.ready else wide_piece]
        width = self.ins[1].shape[-1]
        size = wide_in.shape[1] if self.ready else n * wide_piece.shape[1]
        rows = size // n
        attn_shape = attn_piece.shape[1:]
        self.outs = [
            jax.ShapeDtypeStruct((SEQ, 4) + attn_shape, BF16),
            jax.ShapeDtypeStruct((SEQ, 2, rows, width), BF16),
        ]
        dma = pltpu.SemaphoreType.DMA
        self.scratch = [
            pltpu.VMEM((SEQ, n) + attn_shape, BF16),
            pltpu.VMEM((SEQ, size, width), BF16),
            pltpu.VMEM((2, n // 2, rows, width), BF16),
            pltpu.VMEM((size, SEQ * size), F32),
            pltpu.VMEM((size, SEQ * size), BF16),
            pltpu.VMEM((size, size), F32),
            pltpu.VMEM((size, size), BF16),
            pltpu.VMEM((size, size), BF16),
            pltpu.VMEM((size, 1), F32),
            pltpu.VMEM((1, 1), F32),
            dma((SEQ * n,)),
            dma((6,)),
            dma((2, n // 2)),
            dma((2, n // 2)),
            dma((6, 3)),
            dma((6, 3)),
            dma,
            dma((SEQ,)),
        ]
        self.scratch += OwnerMail.scratch(n, 4)
        if not self.ready:
            self.scratch += OwnerMail.scratch(n, 2) + [pltpu.VMEM((SEQ, size, width), BF16)]

    def run(
        self, attn, wide, attn_orth, wide_orth, attn_in, wide_out, relayed, x32, xlow, gram, gram_low, poly, diag,
        norm, back_s, back_r, relay_s, relay_r, seq_s, seq_r, own, loads, *mails,
    ):
        n = self.n
        b, s, hi, lo, m = coords(n)
        far, near = (s + 2) % 4, s + 1 - 2 * (s % 2)
        me = s * n + b
        size = x32.shape[0]
        width = wide.shape[-1]
        quarter = width // SEQ
        places = owner_list(n)
        attn_mail = OwnerMail(n, places[:4], attn_in, *mails[:3])
        wide_in = wide
        if not self.ready:
            wide_in = mails[6]
            wide_mail = OwnerMail(n, places[4:], wide_in, *mails[3:6])
        mine = [(b == ob) & (s == os) for ob, os in places]
        number = jnp.int32(0)
        for k in range(6):
            number = jnp.where(mine[k], jnp.int32(k), number)
        is_attn = mine[0] | mine[1] | mine[2] | mine[3]
        is_wide = mine[4] | mine[5]

        if not self.ready:
            for k in range(2):
                wide_mail.send(k, wide.at[k])
        def send_attn():
            for k in range(4):
                attn_mail.send(k, attn.at[k])

        if self.ready:
            self.send_attn = send_attn
        else:
            send_attn()

        if not self.ready:
            for _ in range(4):
                yield


        def result(k):
            return attn_orth.at[s, k] if k < 4 else wide_orth.at[s, k - 4]

        def others(act):
            @pl.loop(1, SEQ * n)
            def _(k):
                other = (me + 9 * k) % (SEQ * n)
                act(other, other % n, other // n)

        def give_attn():
            pltpu.make_async_copy(attn_in.at[s, b], attn_orth.at[s, number], own).start()

            def act(other, ob, os):
                remote(
                    attn_in.at[os, ob], attn_orth.at[os, number], back_s.at[other], back_r.at[number], (ob, os)
                ).start()

            others(act)

        piece = OwnerMail(n, places, wide_out, None, None, None).slot

        def give_wide(piece):
            index = number - 4
            pltpu.make_async_copy(piece(s, b), wide_orth.at[s, index], own).start()

            def act(other, ob, os):
                oh, ol = ob // 2, ob % 2
                up = hi < m // 2
                away = jnp.where(up, oh - hi, hi - oh)
                relay = (away > 0) & (os // 2 != s // 2)
                stop = jnp.where(ol == lo, os, (os + 2) % 4)
                src = piece(os, ob)

                @pl.when(relay)
                def _():
                    slot = jnp.maximum(away - 1, 0)
                    remote(
                        src, relayed.at[index, slot], back_s.at[other], relay_r.at[index, slot],
                        (hi * 2 + ol, stop),
                    ).start()

                @pl.when(jnp.logical_not(relay))
                def _():
                    remote(
                        src, wide_orth.at[os, index], back_s.at[other], back_r.at[number], (ob, os)
                    ).start()

            others(act)

        def prepare():
            @pl.when(is_wide)
            def _():
                if not self.ready:
                    wide_mail.collect()
                if width != size:
                    xlow[...] = jnp.zeros(xlow.shape, BF16)

            @pl.when(mine[4])
            def _():
                copies = [
                    pltpu.make_async_copy(
                        wide_in.at[k], xlow.at[:, pl.ds(k * size, width)], loads.at[k]
                    )
                    for k in range(SEQ)
                ]
                for c in copies:
                    c.start()
                for c in copies:
                    c.wait()

            @pl.when(mine[5])
            def _():
                copies = [
                    pltpu.make_async_copy(wide_in.at[k], wide_out.at[k], loads.at[k]) for k in range(SEQ)
                ]
                for c in copies:
                    c.start()
                for k, c in enumerate(copies):
                    c.wait()
                    xlow[:width, k * size : (k + 1) * size] = wide_out[k].T

        def attn_turn():
            @pl.when(is_attn)
            def _():
                attn_mail.collect()
                span = SEQ * quarter
                short, line = attn_in.shape[2:]
                whole = [attn_in[k].reshape(n * short, line) for k in range(SEQ)]
                for k in range(line // quarter):
                    block = [a[:, k * quarter : (k + 1) * quarter] for a in whole]
                    xlow[k * n * short : (k + 1) * n * short, :span] = jnp.concatenate(block, axis=1)
                square_x, square_low = x32.at[:, pl.ds(0, span)], xlow.at[:, pl.ds(0, span)]

                def turn(first):
                    schulz_poly(square_low, gram, gram_low, poly, diag, norm, first)
                    schulz_move(square_x, square_low, poly, diag, norm, first)

                turn(True)

                @pl.loop(1, NS)
                def _(k):
                    turn(False)

                for k in range(SEQ):
                    block = xlow[:, k * quarter : (k + 1) * quarter]
                    if line > quarter:
                        block = fold(block)
                    attn_in[k] = block.reshape(attn_in.shape[1:])
                give_attn()

        if not self.ready:
            prepare()
        else:
            self.prepare, self.attn_turn = prepare, attn_turn
            yield

        for turn in range(NS):

            @pl.when(is_wide)
            def _(turn=turn):
                schulz_poly(xlow, gram, gram_low, poly, diag, norm, turn == 0)

            yield

            @pl.when(is_wide)
            def _(turn=turn):
                schulz_move(x32, xlow, poly, diag, norm, turn == 0)

            yield

        @pl.when(is_wide)
        def _():
            @pl.when(mine[4])
            def _():
                rows = size // n

                def part(seq, block):
                    return xlow.at[
                        pl.ds(pl.multiple_of(block * rows, rows), rows),
                        pl.ds(pl.multiple_of(seq * size, 128), width),
                    ]

                give_wide(part)

            @pl.when(mine[5])
            def _():
                for k in range(SEQ):
                    wide_out[k] = xlow[:width, k * size : (k + 1) * size].T
                give_wide(piece)

        def routes(k):
            ob, os = places[k]
            oh, ol = ob // 2, ob % 2
            same_x = s // 2 == os // 2
            here = (hi == oh) & (((lo == ol) & jnp.logical_not(same_x)) | ((lo != ol) & same_x))
            target = jnp.where(lo == ol, s, far)
            ahead = range(oh + 1, m) if oh < m // 2 else range(oh - 1, -1, -1)
            return here, target, list(enumerate(ahead))

        def relay_copy(k, slot, block, target):
            return remote(
                relayed.at[k - 4, slot], wide_orth.at[target, k - 4], relay_s.at[k - 4, slot], back_r.at[k],
                (block * 2 + lo, target),
            )

        def onward(k, step, source, target):
            out = attn_orth.at[source, k] if k < 4 else wide_orth.at[source, k - 4]
            return remote(out, out, seq_s.at[k, step], seq_r.at[k, step], (b, target))

        if not self.ready:
            attn_turn()
        done = (0, 1, 2, 3, 4, 5)

        def returned(k):
            @pl.when(jnp.logical_not(mine[k]))
            def _():
                remote(result(k), result(k), seq_s.at[k, 0], back_r.at[k], (0, 0)).wait_recv()

            @pl.when(mine[k])
            def _():
                pltpu.make_async_copy(result(k), result(k), own).wait()

            onward(k, 0, s, far).start()
            onward(k, 1, s, near).start()

        def passed(k):
            onward(k, 0, far, far).wait_recv()
            onward(k, 2, far, near).start()

        for k in (4, 5):
            here, target, ahead = routes(k)

            @pl.when(here)
            def _(k=k, target=target, ahead=ahead):
                for slot, block in ahead:
                    place = relayed.at[k - 4, slot]
                    remote(place, place, relay_s.at[0, 0], relay_r.at[k - 4, slot], (0, 0)).wait_recv()
                    relay_copy(k, slot, block, target).start()

        for k in done[:4]:
            returned(k)
        for k in done[4:]:
            returned(k)
        for k in done:
            passed(k)
        for k in done:
            onward(k, 1, near, near).wait_recv()
            onward(k, 2, (near + 2) % 4, near).wait_recv()
            onward(k, 0, s, far).wait_send()
            onward(k, 1, s, near).wait_send()
            onward(k, 2, far, near).wait_send()
        for k in range(4):
            attn_mail.finish(k, attn.at[k])
        if not self.ready:
            for k in range(2):
                wide_mail.finish(k, wide.at[k])
        for k in (4, 5):
            here, target, ahead = routes(k)

            @pl.when(here)
            def _(k=k, target=target, ahead=ahead):
                for slot, block in ahead:
                    relay_copy(k, slot, block, target).wait_send()

        def given(buf):
            def act(other, ob, os):
                place = buf.at[os, ob] if len(buf.shape) == 4 else piece(os, ob)
                remote(place, place, back_s.at[other], back_r.at[0], (0, 0)).wait_send()

            others(act)

        @pl.when(is_attn)
        def _():
            given(attn_in)

        @pl.when(is_wide)
        def _():
            given(wide_out)


def schulz_poly(xlow, gram, gram_low, poly, diag, norm, first):
    size = xlow.shape[0]
    side = 256
    tiles = [slice(k, k + side) for k in range(0, size, side)]
    eye = lax.broadcasted_iota(jnp.int32, (side, side), 0) == lax.broadcasted_iota(
        jnp.int32, (side, side), 1
    )
    for j in tiles:
        gram[j.start :, j] = contract_last(xlow[j.start :, :], xlow[j, :])
    if first:
        total = jnp.zeros((1, 1), F32)
        for j in tiles:
            total = total + jnp.sum(jnp.where(eye, gram[j, j], 0.0), keepdims=True)
        inverse = 1.0 / (jnp.sqrt(total) + tiny_norm)
        norm[...] = inverse
        for j in tiles:
            gram[j.start :, j] = gram[j.start :, j] * (inverse * inverse)
    down, along = [], []
    for j in tiles:
        block = gram[j, j]
        on_diag = jnp.where(eye, block, 0.0)
        down.append(jnp.sum(on_diag, axis=1, keepdims=True))
        along.append(jnp.sum(on_diag, axis=0, keepdims=True))
        gram_low[j, j] = jnp.where(eye, 0.0, block).astype(BF16)
        for i in tiles:
            if i.start > j.start:
                block = gram[i, j]
                gram_low[i, j] = block.astype(BF16)
                gram_low[j, i] = block.T.astype(BF16)
    for j, right in zip(tiles, along):
        square = matmul(gram_low[j.start :, :], gram_low[:, j])
        for i, left in zip(tiles, down):
            if i.start < j.start:
                continue
            part = square[i.start - j.start : i.stop - j.start]
            factor = (2.0315 * left - 4.775) + 2.0315 * right
            block = 2.0315 * part + factor * gram[i, j]
            if i == j:
                value = jnp.sum(jnp.where(eye, 2.0315 * part, 0.0), axis=1, keepdims=True)
                diag[i] = value + (3.4445 + (2.0315 * left - 4.775) * left)
                poly[i, i] = jnp.where(eye, 0.0, block).astype(BF16)
            else:
                poly[i, j] = block.astype(BF16)
                poly[j, i] = block.T.astype(BF16)


def schulz_move(x32, xlow, poly, diag, norm, first):
    wide = x32.shape[1]
    chunk = 768 if wide % 768 == 0 else 512
    for c in range(0, wide, chunk):
        part = slice(c, c + chunk)
        if first:
            moved = (diag[...] * norm[...]) * xlow[:, part].astype(F32)
            moved = moved + matmul(poly[...], xlow[:, part]) * norm[...]
        else:
            moved = diag[...] * x32[:, part] + matmul(poly[...], xlow[:, part])
        x32[:, part] = moved
        xlow[:, part] = moved.astype(BF16)


def greet_peers(n, kinds):
    b, s, hi, lo, m = coords(n)
    peers = []
    if "seq" in kinds:
        peers += [(b, (s + k) % 4) for k in (1, 2, 3)]
    if "batch" in kinds:
        peers += [(((hi + d) % m) * 2 + lo, s) for d in range(1, m)]
        peers += [(hi * 2 + 1 - lo, s)]
    return peers


def greet_signal(n, kinds):
    b, s = lax.axis_index("batch"), lax.axis_index("seq")
    barrier = pltpu.get_barrier_semaphore()
    if "all" in kinds:
        me = s * n + b

        @pl.loop(1, SEQ * n)
        def _(k):
            other = (me + k) % (SEQ * n)
            pl.semaphore_signal(
                barrier, inc=1, device_id=(other % n, other // n), device_id_type=MESH
            )

        return
    for peer in greet_peers(n, kinds):
        pl.semaphore_signal(barrier, inc=1, device_id=peer, device_id_type=MESH)


def greet_wait(n, kinds):
    count = SEQ * n - 1 if "all" in kinds else len(greet_peers(n, kinds))
    pl.semaphore_wait(pltpu.get_barrier_semaphore(), count)


def greet(n, kinds):
    greet_signal(n, kinds)
    greet_wait(n, kinds)


def run_together(*live):
    live = list(live)
    while live:
        still = []
        for op in live:
            try:
                next(op)
                still.append(op)
            except StopIteration:
                pass
        live = still


def exchange(n, collective_id, name, *ops):
    ins = [a for op in ops for a in op.ins]
    outs = [o for op in ops for o in op.outs]
    scratch = [c for op in ops for c in op.scratch]
    kinds = {k for op in ops for k in op.peers}

    def kernel(*refs):
        in_refs, out_refs = refs[: len(ins)], refs[len(ins) : len(ins) + len(outs)]
        scratch_refs = refs[len(ins) + len(outs) :]
        greet(n, kinds)
        live = []
        i = o = c = 0
        for op in ops:
            ni, no, nc = len(op.ins), len(op.outs), len(op.scratch)
            live.append(
                op.run(*in_refs[i : i + ni], *out_refs[o : o + no], *scratch_refs[c : c + nc])
            )
            i, o, c = i + ni, o + no, c + nc
        run_together(*live)

    vmem = pl.BlockSpec(memory_space=pltpu.VMEM)
    return pl.pallas_call(
        kernel,
        out_shape=outs,
        in_specs=[vmem] * len(ins),
        out_specs=[vmem] * len(outs),
        scratch_shapes=scratch,
        compiler_params=pltpu.CompilerParams(
            collective_id=collective_id, has_side_effects=True, vmem_limit_bytes=60 * 2**20
        ),
        name=name,
    )(*ins)


def contract_last(left, right):
    return lax.dot_general(left, right, (((1,), (1,)), ((), ())), preferred_element_type=F32)


def contract_first(left, right):
    return lax.dot_general(left, right, (((0,), (0,)), ((), ())), preferred_element_type=F32)


def matmul(left, right):
    return jnp.dot(left, right, preferred_element_type=F32)


def exact_gelu(value_in):
    return jax.nn.gelu(value_in, approximate=False)


def normalize(hidden, gain_row):
    row_mean = jnp.mean(hidden, axis=-1, keepdims=True)
    centred = hidden - row_mean
    spread = lax.rsqrt(jnp.mean(centred * centred, axis=-1, keepdims=True) + norm_eps)
    scaled = centred * spread
    return (scaled * gain_row, scaled, spread)


def normalize_back(grad_in, scaled, spread, gain_row):
    weighted = grad_in * gain_row
    mean_first = jnp.mean(weighted, axis=-1, keepdims=True)
    second = jnp.mean(weighted * scaled, axis=-1, keepdims=True)
    return (
        spread * (weighted - mean_first - scaled * second),
        jnp.sum(grad_in * scaled, axis=0),
        jnp.sum(grad_in, axis=0),
    )


class RowGather:
    @staticmethod
    def scratch():
        return [pltpu.SemaphoreType.DMA((2, 3)), pltpu.SemaphoreType.DMA((2, 3))]

    def __init__(self, buf, ss, rs):
        self.buf, self.ss, self.rs = buf, ss, rs
        self.b, self.s = lax.axis_index("batch"), lax.axis_index("seq")
        self.far, self.near = (self.s + 2) % 4, self.s + 1 - 2 * (self.s % 2)
        self.diag = (self.near + 2) % 4

    def copy(self, r, step, block, device):
        place = self.buf.at[r, block]
        return remote(place, place, self.ss.at[r, step], self.rs.at[r, step], (self.b, device))

    def start(self, r):
        self.copy(r, 0, self.s, self.far).start()
        self.copy(r, 1, self.s, self.near).start()

    def wait_near(self, r):
        self.copy(r, 1, self.near, self.near).wait_recv()

    def pass_far(self, r):
        self.copy(r, 0, self.far, self.far).wait_recv()
        self.copy(r, 2, self.far, self.near).start()

    def wait_diag(self, r):
        self.copy(r, 2, self.diag, self.near).wait_recv()

    def finish(self, r):
        self.copy(r, 0, self.s, self.far).wait_send()
        self.copy(r, 1, self.s, self.near).wait_send()
        self.copy(r, 2, self.far, self.near).wait_send()


def gelu_parts(value):
    cdf = 0.5 * (1.0 + lax.erf(value * math.sqrt(0.5)))
    density = jnp.exp(-0.5 * value * value) * (1.0 / math.sqrt(2.0 * math.pi))
    return value * cdf, cdf + value * density


def row_sum(value):
    return jnp.sum(value, axis=0, keepdims=True)


class RowSwap:
    @staticmethod
    def scratch(shape):
        return [
            pltpu.VMEM(shape, BF16),
            pltpu.VMEM(shape, BF16),
            pltpu.SemaphoreType.DMA((2, 4)),
            pltpu.SemaphoreType.DMA((2, 4)),
        ]

    def __init__(self, src, dst, ss, rs):
        self.src, self.dst, self.ss, self.rs = src, dst, ss, rs
        self.b, self.s = lax.axis_index("batch"), lax.axis_index("seq")

    def copy(self, r, k):
        other = (self.s + k) % 4
        return remote(
            self.src.at[other, r], self.dst.at[self.s, r], self.ss.at[r, k], self.rs.at[r, k],
            (self.b, other),
        )

    def start(self, r):
        for k in (2, 3, 1):
            self.copy(r, k).start()
        self.dst[self.s, r] = self.src[self.s, r]

    def wait(self, r):
        for k in (2, 3, 1):
            self.copy(r, k).wait_recv()

    def finish(self, r):
        for k in (2, 3, 1):
            self.copy(r, k).wait_send()


def fold(value):
    half = value.shape[0] // 2
    return jnp.concatenate([value[:half], value[half:]], axis=1)


def unfold(value):
    half = value.shape[1] // 2
    return jnp.concatenate([value[:, :half], value[:, half:]], axis=0)


def rounds(count):
    for _ in range(count):
        yield


def spaced(op, count):
    for _ in op:
        yield from rounds(count)


def step(op):
    try:
        next(op)
    except StopIteration:
        pass


def drain(op):
    for _ in op:
        pass


class DirectSum:
    peers = ("all",)

    def __init__(self, n, src):
        self.n = n
        self.scratch = [pltpu.VMEM(src.shape, F32)] + [pltpu.SemaphoreType.DMA((n,))] * 2

    def run(self, src, dst, arrived, ss, rs):
        n = self.n
        b, s = lax.axis_index("batch"), lax.axis_index("seq")
        copies = []
        for k in range(1, n):
            to = (b + k) % n
            copies.append(remote(src.at[to], arrived.at[k], ss.at[k], rs.at[k], (to, s)))
            copies[-1].start()
        yield
        total = src[b]
        for k, c in enumerate(copies):
            c.wait()
            total = total + arrived[k + 1]
        dst[...] = total


class BatchSum:
    peers = ("batch",)

    def __init__(self, n, src):
        self.n = n
        self.ins = [src]
        shape = src.shape[1:]
        self.outs = [jax.ShapeDtypeStruct(shape, F32)]
        m = n // 2
        self.scratch = [pltpu.VMEM((m,) + shape, BF16)] * 3 + [pltpu.SemaphoreType.DMA((m,))] * 4

    def run(self, src, dst, yrecv, zsend, zrecv, ys, yr, zs, zr):
        b, s, hi, lo, m = coords(self.n)
        pair = (hi * 2 + 1 - lo, s)
        first = {}
        for d in list(range(1, m)) + [0]:
            block = ((hi + d) % m) * 2 + 1 - lo
            first[d] = remote(src.at[block], yrecv.at[d], ys.at[d], yr.at[d], pair)
            first[d].start()
        yield
        second = []
        for d in range(1, m):
            h = (hi + d) % m
            first[d].wait_recv()
            zsend[d] = (src[h * 2 + lo].astype(F32) + yrecv[d].astype(F32)).astype(BF16)
            c = remote(zsend.at[d], zrecv.at[d], zs.at[d], zr.at[d], (h * 2 + lo, s))
            c.start()
            second.append(c)
            yield
        first[0].wait_recv()
        total = src[b].astype(F32) + yrecv[0].astype(F32)
        for d in range(1, m):
            second[d - 1].wait_recv()
            total = total + zrecv[d].astype(F32)
        dst[...] = total
        for c in list(first.values()) + second:
            c.wait_send()


class RowSum:
    @staticmethod
    def scratch(rows, shape):
        return [
            pltpu.VMEM((rows, 2) + shape, BF16),
            pltpu.VMEM((rows,) + shape, BF16),
            pltpu.VMEM((rows,) + shape, BF16),
            pltpu.SemaphoreType.DMA((rows, 3)),
            pltpu.SemaphoreType.DMA((rows, 3)),
        ]

    def __init__(self, src, near_in, far_out, far_in, ss, rs):
        self.src, self.near_in, self.far_out, self.far_in, self.ss, self.rs = (
            src, near_in, far_out, far_in, ss, rs,
        )
        self.b, self.s = lax.axis_index("batch"), lax.axis_index("seq")
        self.far, self.near = (self.s + 2) % 4, self.s + 1 - 2 * (self.s % 2)
        self.diag = (self.near + 2) % 4

    def beside(self, r, k):
        block = self.diag if k else self.near
        return remote(
            self.src.at[r, block], self.near_in.at[r, k], self.ss.at[r, k], self.rs.at[r, k],
            (self.b, self.near),
        )

    def across(self, r):
        return remote(
            self.far_out.at[r], self.far_in.at[r], self.ss.at[r, 2], self.rs.at[r, 2],
            (self.b, self.far),
        )

    def send_near(self, r):
        self.beside(r, 0).start()

    def send_diag(self, r):
        self.beside(r, 1).start()

    def cross(self, r):
        self.beside(r, 1).wait_recv()
        part = self.src[r, self.far].astype(F32) + self.near_in[r, 1].astype(F32)
        self.far_out[r] = part.astype(BF16)
        self.across(r).start()

    def total(self, r):
        self.beside(r, 0).wait_recv()
        part = self.src[r, self.s].astype(F32) + self.near_in[r, 0].astype(F32)
        self.across(r).wait_recv()
        return part + self.far_in[r].astype(F32)

    def finish(self, r):
        self.beside(r, 0).wait_send()
        self.beside(r, 1).wait_send()
        self.across(r).wait_send()


class Scratch:
    def __init__(self):
        self.names, self.shapes = [], []

    def add(self, **named):
        for name, shapes in named.items():
            one = not isinstance(shapes, list)
            shapes = [shapes] if one else shapes
            self.names.append((name, len(shapes), one))
            self.shapes += shapes

    def refs(self, refs):
        out, i = types.SimpleNamespace(), 0
        for name, count, one in self.names:
            setattr(out, name, refs[i] if one else refs[i : i + count])
            i += count
        return out


def layer(
    n, tokens, attn_weight, up_weight, down_weight, vec_own, pool_own, lengths, out_grad, up_moment, down_moment
):
    rows, span, width = tokens.shape
    quarter = width // SEQ
    span_all = span * SEQ
    own_rows = width // n
    local = rows * span
    aligned = own_rows % 16 == 0
    scale = HD**-0.5
    shape = jax.ShapeDtypeStruct
    full = (rows, SEQ, span, width)
    widths = (3 * quarter, quarter, width, width)
    low_ops = [GatherBatch(n, shape((own_rows, c), BF16), k < 2) for k, c in enumerate(widths)]
    low_ops = low_ops if aligned else []
    vec_op = GatherDirect(n, vec_own) if aligned else GatherBatch(n, vec_own)
    pool_op = GatherSeq(n, pool_own)
    out_op = GatherSeq(n, shape((width, quarter), BF16))
    sum_ops = [BatchSum(n, shape((n, own_rows, width), BF16)) for _ in range(2)]

    outs = [
        shape((rows, span, width), F32),
        shape((rows, width), F32),
        shape((rows, span, width), F32),
        shape((8, width), F32),
        shape((1, 3 * quarter), F32),
        shape(full, BF16),
    ]
    vmem = pl.BlockSpec(memory_space=pltpu.VMEM)
    anywhere = pl.BlockSpec(memory_space=pl.ANY)
    if aligned:
        outs += [shape((n, own_rows, width), BF16)]
        outs += [shape((2, own_rows, width), BF16), shape((SEQ, width, width), BF16)]
        out_specs = [anywhere, vmem, anywhere, vmem, vmem, anywhere, anywhere, vmem, anywhere]
    else:
        outs += [shape((width, width), BF16)] * 3
        out_specs = [vmem] * 9

    dma = pltpu.SemaphoreType.DMA
    sc = Scratch()
    if aligned:
        sc.add(
            lows=[pltpu.VMEM((own_rows, c), BF16) for c in widths],
            weights=[pltpu.VMEM(op.outs[0].shape, BF16) for op in low_ops],
            low_moves=[c for op in low_ops for c in op.scratch],
        )
    sc.add(vec_parts=pltpu.VMEM(vec_op.outs[0].shape, F32))
    sc.add(vec_move=vec_op.scratch)
    sc.add(vec=pltpu.VMEM((8, width), F32))
    sc.add(pool_parts=pltpu.VMEM(pool_op.outs[0].shape, F32))
    sc.add(pool_move=pool_op.scratch)
    sc.add(out_own=pltpu.VMEM((width, quarter), BF16))
    sc.add(out_parts=pltpu.VMEM((SEQ, width, quarter), BF16))
    sc.add(out_move=out_op.scratch)
    sc.add(w_out=pltpu.VMEM((width, width), BF16))
    sc.add(x_all=pltpu.VMEM(full, BF16))
    sc.add(x_gather=RowGather.scratch())
    sc.add(qkv=pltpu.VMEM((rows, span_all, 3 * quarter), BF16))
    sc.add(prob=pltpu.VMEM((rows, HEADS, span_all, span_all), F32))
    sc.add(swap=RowSwap.scratch((SEQ, rows, span, quarter)))
    sc.add(back_swap=RowSwap.scratch((SEQ, rows, span, quarter)))
    sc.add(context=pltpu.VMEM((rows, span, width), BF16))
    sc.add(normed=pltpu.VMEM((rows, span, width), F32))
    sc.add(scaled_one=pltpu.VMEM((rows, span, width), F32))
    sc.add(spread_one=pltpu.VMEM((rows, span, 1), F32))
    sc.add(y_all=pltpu.VMEM(full, BF16))
    sc.add(y_gather=RowGather.scratch())
    sc.add(slope=pltpu.VMEM(full, F32))
    sc.add(act=pltpu.VMEM(full, BF16))
    sc.add(z_sum=RowSum.scratch(rows, (span, width)))
    sc.add(dz_all=pltpu.VMEM(full, BF16))
    sc.add(dz_gather=RowGather.scratch())
    sc.add(du_all=pltpu.VMEM(full, BF16))
    sc.add(dy_sum=RowSum.scratch(rows, (span, width)))
    sc.add(pool_buf=pltpu.VMEM((SEQ, rows, width), F32))
    sc.add(pool_sems=[dma((3,)), dma((3,))])
    sc.add(a_quarters=pltpu.VMEM((SEQ, local, quarter), BF16))
    sc.add(out_part=pltpu.VMEM((1, SEQ, width, quarter), BF16))
    sc.add(out_sum=RowSum.scratch(1, (width, quarter)))
    if not aligned:
        sc.add(x_sum=RowSum.scratch(rows, (span, width)))
    sc.add(grad_qkv=pltpu.VMEM((rows, span_all, 3 * quarter), BF16))
    if aligned:
        sc.add(early=[pltpu.VMEM(outs[k].shape, outs[k].dtype) for k in (0, 2, 5, 6)])
        sc.add(early_sems=dma((4,)))
        sc.add(raw=dma((2 * SEQ + 1,)))
        sc.add(
            down_grad=pltpu.VMEM((n, own_rows, width), BF16),
            up_grad=pltpu.VMEM((n, own_rows, width), BF16),
            down_piece=pltpu.VMEM((own_rows, width), F32),
            up_piece=pltpu.VMEM((own_rows, width), F32),
            down_sum=sum_ops[0].scratch,
            up_sum=sum_ops[1].scratch,
        )
        sc.add(vec_low=pltpu.VMEM(vec_own.shape, F32))
        sc.add(wide_send=pltpu.VMEM((2, own_rows, width), BF16))
        sc.add(mail=OwnerMail.scratch(n, 2, (own_rows, width)))

    def kernel(
        tokens, attn_weight, up_weight, down_weight, vec_own, pool_own, lengths, out_grad, up_moment, down_moment,
        out_rows, pooled, second, vec_grad, bias_sums, part, grad_attn, *rest,
    ):
        if aligned:
            wide_bf, wide_in = rest[:2]
            rest = rest[2:]
        else:
            grad_up_out, grad_down_out = rest[:2]
            rest = rest[2:]
        at = sc.refs(rest)
        if aligned:
            leaving = [
                pltpu.make_async_copy(a, b, at.early_sems.at[k])
                for k, (a, b) in enumerate(zip(at.early, (out_rows, second, part, grad_attn)))
            ]
            out_rows, second, part, grad_attn = at.early
        kinds = {"all"} if aligned else {"seq", "batch"}
        greet_signal(n, kinds)
        b, s = lax.axis_index("batch"), lax.axis_index("seq")
        x_all, y_all, dz_all, du_all = at.x_all, at.y_all, at.dz_all, at.du_all
        slope, act, prob, qkv = at.slope, at.act, at.prob, at.qkv
        normed, context, vec = at.normed, at.context, at.vec
        x_gather = RowGather(x_all, *at.x_gather)
        y_gather = RowGather(y_all, *at.y_gather)
        dz_gather = RowGather(dz_all, *at.dz_gather)
        swap, back_swap = RowSwap(*at.swap), RowSwap(*at.back_swap)
        z_sum, dy_sum = [RowSum(part, *refs) for refs in (at.z_sum, at.dy_sum)]
        out_sum = RowSum(at.out_part, *at.out_sum)
        far, near, diag = x_gather.far, x_gather.near, x_gather.diag

        def raw_block(k):
            return slope.at[k // SEQ, k % SEQ, pl.ds(0, own_rows)]

        def load_up(matrix):
            return [
                pltpu.make_async_copy(
                    matrix.at[:, pl.ds(k * width, width)], raw_block(SEQ + k), at.raw.at[SEQ + k]
                )
                for k in range(SEQ)
            ]

        def load_down(matrix, place):
            return pltpu.make_async_copy(
                matrix.at[pl.ds(s * own_rows, own_rows)], place, at.raw.at[2 * SEQ]
            )

        def raw_up(k):
            whole = jnp.concatenate([raw_block(SEQ + j)[...] for j in range(SEQ)], axis=1)
            return take_up(whole, n, k)

        if aligned:
            raws = [
                pltpu.make_async_copy(attn_weight.at[k], raw_block(k), at.raw.at[k]) for k in range(4)
            ]
            raws += load_up(up_weight)
            raws.append(load_down(down_weight, second.at[0, pl.ds(0, own_rows)]))
            for c in raws:
                c.start()
        for r in range(rows):
            x_all[r, s] = tokens[r].astype(BF16)
        if aligned:
            for c in raws[:4]:
                c.wait()
            for k in range(SEQ):

                @pl.when(s == k)
                def _(k=k):
                    block = [raw_block(j)[:, k * quarter : (k + 1) * quarter] for j in range(4)]
                    at.lows[0][...] = jnp.concatenate(block[:3], axis=1).astype(BF16)
                    at.lows[1][...] = block[3].astype(BF16)

            vec_low = at.vec_low
            vec_low[...] = vec_own[...].astype(BF16).astype(F32)
        else:
            vec_low = vec_own

        greet_wait(n, kinds)
        vec_move = vec_op.run(vec_low, at.vec_parts, *at.vec_move)
        pool_move = pool_op.run(pool_own, at.pool_parts, *at.pool_move)
        step(vec_move)
        if aligned:
            moves = [
                op.run(at.lows[k], at.weights[k], *at.low_moves[5 * k : 5 * k + 5])
                for k, op in enumerate(low_ops)
            ]
            step(moves[0])
        step(pool_move)
        for r in range(rows):
            x_gather.start(r)
        if aligned:
            for c in raws[4:]:
                c.wait()
            for k in range(SEQ):

                @pl.when(s == k)
                def _(k=k):
                    at.lows[2][...] = raw_up(k).astype(BF16)

            at.lows[3][...] = second[0, :own_rows].astype(BF16)
            step(moves[0])
        x_gather.pass_far(0)
        if aligned:
            step(moves[0])
        step(pool_move)
        x_gather.pass_far(1)
        if aligned:
            step(moves[0])
            step(moves[1])
            step(moves[2])
        drain(vec_move)
        drain(pool_move)
        if aligned:
            whole = jnp.concatenate([at.vec_parts[k] for k in range(n)], axis=1)

            def here(make):
                return sum(jnp.where(s == k, make(k), 0.0) for k in range(SEQ))

            vec[0:6] = whole[2:8]
            vec[6:7] = here(
                lambda k: jnp.concatenate(
                    [
                        whole[8 + f // width : 9 + f // width, f % width : f % width + own_rows]
                        for f in ((j * SEQ + k) * own_rows for j in range(n))
                    ],
                    axis=1,
                )
            )
            blank = jnp.zeros((1, quarter), F32)
            vec[7:8] = here(
                lambda k: jnp.concatenate(
                    [
                        whole[0:1, k * quarter : (k + 1) * quarter],
                        blank,
                        whole[1:2, k * quarter : (k + 1) * quarter],
                        blank,
                    ],
                    axis=1,
                )
            )
        else:
            total = at.vec_parts[0]
            for k in range(1, n):
                total = total + at.vec_parts[k]
            vec[...] = total
        pool_whole = jnp.concatenate([at.pool_parts[k] for k in range(SEQ)], axis=1)

        if aligned:
            drain(moves[0])
            step(moves[1])
            step(moves[2])
            step(moves[3])

        def w_qkv():
            if aligned:
                return at.weights[0][...].reshape(width, 3 * quarter)
            return attn_weight[:, : 3 * quarter]

        def w_up():
            return at.weights[2][...].reshape(width, width) if aligned else up_weight[...]

        def w_down():
            return at.weights[3][...].reshape(width, width) if aligned else down_weight[...]

        out_move = out_op.run(at.out_own, at.out_parts, *at.out_move)

        def begin_out():
            if aligned:
                drain(moves[1])
                at.out_own[...] = at.weights[1][...].reshape(width, quarter)
            else:
                at.out_own[...] = attn_weight[:, 3 * quarter :]
            step(out_move)

        def turn(*ks):
            for k in ks:
                if aligned:
                    step(moves[k])

        bias = vec[7:8, : 3 * quarter]
        column = lax.broadcasted_iota(jnp.int32, (1, span_all), 1)

        def heads(r, h):
            return [
                qkv[r, :, k * quarter + h * HD : k * quarter + (h + 1) * HD] for k in range(3)
            ]

        for r in range(rows):
            x_gather.wait_near(r)
            x_gather.wait_diag(r)
            block = matmul(x_all[r].reshape(span_all, width), w_qkv()) + bias
            qkv[r] = block.astype(BF16)
            valid = column < lengths[r]
            if r == 0:
                turn(1)
            mixed = []
            for h in range(HEADS):
                query, key, value = heads(r, h)
                scores = contract_last(query * jnp.bfloat16(scale), key)
                scores = jnp.where(valid, scores, -1e30)
                exponent = jnp.exp(scores - jnp.max(scores, axis=-1, keepdims=True))
                weight = exponent * (1.0 / jnp.sum(exponent, axis=-1, keepdims=True))
                prob[r, h] = weight
                mixed.append(matmul(weight.astype(BF16), value))
                if r == 0 and h == 0:
                    turn(1, 3, 2)
                if r == 0 and h == 1:
                    begin_out()
                    turn(2)
                if r == 0 and h == 2:
                    turn(2)
                if r == 1:
                    turn(3)
            mixed = jnp.concatenate(mixed, axis=1).astype(BF16)
            for k in range(SEQ):
                at.swap[0][k, r] = mixed[k * span : (k + 1) * span]
            swap.start(r)
        step(out_move)
        drain(out_move)
        w_out = at.w_out
        w_out[...] = jnp.concatenate([at.out_parts[k] for k in range(SEQ)], axis=1)
        gain_one, shift_one = vec[1:2], vec[2:3]
        for r in range(rows):
            swap.wait(r)
            context[r] = jnp.concatenate([at.swap[1][k, r] for k in range(SEQ)], axis=1)
            hidden = tokens[r] + (matmul(context[r], w_out[...]) + vec[0:1])
            centred = hidden - jnp.mean(hidden, axis=-1, keepdims=True)
            spread = lax.rsqrt(jnp.mean(centred * centred, axis=-1, keepdims=True) + norm_eps)
            scaled = centred * spread
            at.scaled_one[r] = scaled
            at.spread_one[r] = spread
            value = scaled * gain_one + shift_one
            normed[r] = value
            y_all[r, s] = value.astype(BF16)
            y_gather.start(r)

        if aligned:
            drain(moves[2])
        gain_two, shift_two = vec[3:4], vec[4:5]
        bias_down, bias_up = vec[5:6], vec[6:7]

        def pair(ref, blocks):
            return jnp.concatenate([ref[i] for i in blocks], axis=0)

        def put(ref, blocks, value):
            for k, i in enumerate(blocks):
                ref[i] = value[k * span : (k + 1) * span].astype(ref.dtype)

        def rise(blocks):
            value, rate = gelu_parts(matmul(pair(y_all, blocks), w_up()) + bias_up)
            put(act, blocks, value)
            put(slope, blocks, rate)

        def fall(blocks):
            put(part, blocks, matmul(pair(act, blocks), w_down()))

        mine, beside = [[(r, k) for r in range(rows)] for k in (s, near)]
        rise(mine)
        for r in range(rows):
            y_gather.wait_near(r)
        rise(beside)
        if aligned:
            drain(moves[3])
        fall(beside)
        for r in range(rows):
            z_sum.send_near(r)
        for r in range(rows):
            y_gather.pass_far(r)
            y_gather.wait_diag(r)
            rise([(r, diag), (r, far)])
            fall([(r, diag), (r, far)])
            z_sum.send_diag(r)
            if r == 0:
                fall(mine)
            z_sum.cross(r)

        position = s * span + lax.broadcasted_iota(jnp.int32, (span, 1), 0)
        grad_gain_two = grad_shift_two = grad_bias_down = jnp.zeros((1, width), F32)
        for r in range(rows):
            hidden = normed[r] + (z_sum.total(r) + bias_down)
            centred = hidden - jnp.mean(hidden, axis=-1, keepdims=True)
            spread_two = lax.rsqrt(jnp.mean(centred * centred, axis=-1, keepdims=True) + norm_eps)
            scaled = centred * spread_two
            output = scaled * gain_two + shift_two
            out_rows[r] = output
            live = (position < lengths[r]).astype(F32)
            length = jnp.full((1, 1), lengths[r], jnp.int32).astype(F32)
            at.pool_buf[s, r : r + 1] = row_sum(output * live) / length
            upstream = live * (out_grad[r] + pool_whole[r : r + 1] / length)
            weighted = upstream * gain_two
            mean_first = jnp.mean(weighted, axis=-1, keepdims=True)
            mean_second = jnp.mean(weighted * scaled, axis=-1, keepdims=True)
            grad = spread_two * (weighted - mean_first - scaled * mean_second)
            second[r] = grad
            low = grad.astype(BF16)
            dz_all[r, s] = low
            dz_gather.start(r)
            grad_gain_two += row_sum(upstream * scaled)
            grad_shift_two += row_sum(upstream)
            grad_bias_down += row_sum(low.astype(F32))

        if aligned:
            leaving[0].start()

        def pool_copy(k, block, device):
            place = at.pool_buf.at[block]
            sems = at.pool_sems
            return remote(place, place, sems[0].at[k - 1], sems[1].at[k - 1], (b, device))

        for k in (1, 2, 3):
            pool_copy(k, s, (s + k) % 4).start()
        for r in range(rows):
            z_sum.finish(r)

        def backward(blocks):
            lift = contract_last(pair(dz_all, blocks), w_down())
            low = (lift * pair(slope, blocks)).astype(BF16)
            put(du_all, blocks, low)
            put(part, blocks, contract_last(low, w_up()))
            return row_sum(low.astype(F32))

        bias_grad = backward(mine)
        for r in range(rows):
            dz_gather.wait_near(r)
        bias_grad += backward(beside)
        for r in range(rows):
            dy_sum.send_near(r)
        for r in range(rows):
            dz_gather.pass_far(r)
            dz_gather.wait_diag(r)
            bias_grad += backward([(r, diag), (r, far)])
            dy_sum.send_diag(r)
            dy_sum.cross(r)

        flat = rows * span_all
        if aligned:
            down_move = sum_ops[0].run(at.down_grad, at.down_piece, *at.down_sum)
            up_move = sum_ops[1].run(at.up_grad, at.up_piece, *at.up_sum)
            mail = OwnerMail(n, owner_list(n)[4:], wide_in, *at.mail)
            wide_send = at.wide_send
            momenta = load_up(up_moment) + [load_down(down_moment, raw_block(0))]
            for c in momenta:
                c.start()
        whole = contract_first(act[...].reshape(flat, width), dz_all[...].reshape(flat, width))
        if aligned:
            at.down_grad[...] = whole.reshape(n, own_rows, width).astype(BF16)
            step(down_move)
        else:
            grad_down_out[...] = whole.astype(BF16)
        whole = contract_first(y_all[...].reshape(flat, width), du_all[...].reshape(flat, width))
        if aligned:
            at.up_grad[...] = whole.reshape(n, own_rows, width).astype(BF16)
            step(up_move)
        else:
            grad_up_out[...] = whole.astype(BF16)

        grad_gain_one = grad_shift_one = grad_bias_out = jnp.zeros((1, width), F32)
        for r in range(rows):
            grad = dy_sum.total(r) + second[r]
            scaled = at.scaled_one[r]
            weighted = grad * gain_one
            mean_first = jnp.mean(weighted, axis=-1, keepdims=True)
            mean_second = jnp.mean(weighted * scaled, axis=-1, keepdims=True)
            first = at.spread_one[r] * (weighted - mean_first - scaled * mean_second)
            second[r] = first
            low = first.astype(BF16)
            above = contract_last(low, w_out[...]).astype(BF16)
            for k in range(SEQ):
                columns = slice(k * quarter, (k + 1) * quarter)
                at.back_swap[0][k, r] = above[:, columns]
                at.a_quarters[k, r * span : (r + 1) * span] = low[:, columns]
            back_swap.start(r)
            grad_gain_one += row_sum(grad * scaled)
            grad_shift_one += row_sum(grad)
            grad_bias_out += row_sum(low.astype(F32))
        for k, value in enumerate(
            (
                grad_bias_out, grad_gain_one, grad_shift_one, grad_gain_two, grad_shift_two,
                grad_bias_down, bias_grad, jnp.zeros((1, width), F32),
            )
        ):
            vec_grad[k : k + 1] = value

        def new_momentum(k, piece, old):
            wide_bf[k] = piece[...].astype(BF16)
            wide_send[k] = (matrix_decay * old + wide_bf[k].astype(F32)).astype(BF16)
            mail.send(k, wide_send.at[k])

        flat_context = context[...].reshape(local, width)
        for k in range(SEQ):
            at.out_part[0, k] = contract_first(flat_context, at.a_quarters[k]).astype(BF16)
        out_sum.send_diag(0)
        out_sum.send_near(0)
        for r in range(rows):
            dy_sum.finish(r)
        sums = jnp.zeros((1, 3 * quarter), F32)
        for r in range(rows):
            back_swap.wait(r)
            arrived = jnp.concatenate([at.back_swap[1][k, r] for k in range(SEQ)], axis=0)
            query_grads, key_grads, value_grads = [], [], []
            for h in range(HEADS):
                query, key, value = heads(r, h)
                above = arrived[:, h * HD : (h + 1) * HD]
                weight = prob[r, h]
                prob_grad = contract_last(above, value)
                delta = jnp.sum(weight * prob_grad, axis=-1, keepdims=True)
                score_grad = (weight * (prob_grad - delta)).astype(BF16)
                query_grads.append(matmul(score_grad, key) * scale)
                key_grads.append(contract_first(query, score_grad) * scale)
                value_grads.append(contract_first(above, weight.astype(BF16)))
                if aligned and r == 0:
                    step(down_move)
                if r == 1 and h == 0:
                    out_sum.cross(0)
                if aligned and r == 1 and h > 0:
                    step(up_move)
                if not aligned and r > 0 and h == 2:
                    x_sum.cross(r - 1)
            turned = jnp.concatenate(key_grads + value_grads, axis=0).T
            block = jnp.concatenate(query_grads + [turned], axis=1).astype(BF16)
            at.grad_qkv[r] = block
            sums += row_sum(block.astype(F32))
            out = contract_last(block, w_qkv())
            for k in range(SEQ):
                part[r, k] = out[k * span : (k + 1) * span].astype(BF16)
            if not aligned:
                if r == 0:
                    x_sum = RowSum(part, *at.x_sum)
                x_sum.send_diag(r)
                x_sum.send_near(r)
        if aligned:
            step(up_move)
            drain(down_move)
            for c in momenta:
                c.wait()
            new_momentum(1, at.down_piece, raw_block(0)[...])
        bias_sums[...] = sums
        if aligned:
            leaving[1].start()
            leaving[2].start()
        whole = contract_first(
            x_all[...].reshape(flat, width), at.grad_qkv[...].reshape(flat, 3 * quarter)
        )
        whole = jnp.concatenate([whole, out_sum.total(0)], axis=1)
        grad_attn[...] = whole.astype(BF16).reshape(grad_attn.shape)
        if aligned:
            leaving[3].start()
        for k in (1, 2, 3):
            pool_copy(k, (s + 4 - k) % 4, (s + k) % 4).wait_recv()
        pool_buf = at.pool_buf
        pooled[...] = (pool_buf[0] + pool_buf[1]) + (pool_buf[2] + pool_buf[3])
        if aligned:
            mail.relay(1)
            drain(up_move)
            for k in range(SEQ):

                @pl.when(s == k)
                def _(k=k):
                    wide_bf[0] = at.up_piece[...].astype(BF16)
                    old = matrix_decay * raw_up(k) + wide_bf[0].astype(F32)
                    wide_send[0] = old.astype(BF16)

            mail.send(0, wide_send.at[0])
        else:
            x_sum.cross(rows - 1)
            for r in range(rows):
                second[r] = x_sum.total(r) + second[r]
                x_sum.finish(r)
        out_sum.finish(0)
        for k in (1, 2, 3):
            pool_copy(k, s, (s + k) % 4).wait_send()
        for r in range(rows):
            for op in (x_gather, swap, y_gather, dz_gather, back_swap):
                op.finish(r)
        if aligned:
            mail.relay(0)

            @pl.when(mail.mine[0] | mail.mine[1])
            def _():
                mail.collect()

            for k in range(2):
                mail.finish(k, wide_send.at[k])
            for c in leaving:
                c.wait()

    smem = pl.BlockSpec(memory_space=pltpu.SMEM)
    far_spec = anywhere if aligned else vmem
    return pl.pallas_call(
        kernel,
        out_shape=outs,
        in_specs=[vmem] + [far_spec] * 3 + [vmem] * 2 + [smem, vmem] + [anywhere] * 2,
        out_specs=out_specs,
        scratch_shapes=sc.shapes,
        compiler_params=pltpu.CompilerParams(
            collective_id=0, has_side_effects=True, vmem_limit_bytes=63 * 2**20
        ),
        name="layer",
    )(tokens, attn_weight, up_weight, down_weight, vec_own, pool_own, lengths, out_grad, up_moment, down_moment)


def join_up_parts(parts, n):
    hid_own = parts[0].shape[1] // n
    return jnp.concatenate(
        [parts[k][:, b * hid_own : (b + 1) * hid_own] for b in range(n) for k in range(SEQ)], axis=1
    )


def take_up(matrix, n, k):
    hid_own = matrix.shape[1] // n // SEQ
    return jnp.concatenate(
        [
            matrix[:, (b * SEQ + k) * hid_own : (b * SEQ + k + 1) * hid_own]
            for b in range(n)
        ],
        axis=1,
    )


def muon(n, grad_attn, wide_in, bias_sums, vec_grad, attn_moment, wide_bf, x_part, first_grad):
    rows, width = wide_bf.shape[1:]
    quarter = width // SEQ
    hid_own = rows
    n_vec = 8 + SEQ
    shape = jax.ShapeDtypeStruct
    attn_shape = (4, rows // 2, 2 * quarter)
    attn_op = GatherSeq(n, shape(attn_shape, BF16))
    attn_sum = BatchSum(n, grad_attn)
    vec_sum = DirectSum(n, shape((n, n_vec, rows), F32))
    vec_op = GatherSeq(n, shape((n_vec, rows), F32))
    wide_op = GatherSeq(n, wide_bf)
    count, span = first_grad.shape[:2]
    main = Muon(n, shape(attn_shape, BF16), wide_in=wide_in)
    outs = [attn_op.outs[0], wide_op.outs[0], shape((n_vec, rows), F32), shape(first_grad.shape, F32)]
    outs += main.outs
    groups = [
        [
            pltpu.VMEM((rows, width), F32),
            pltpu.VMEM(attn_shape, BF16),
            pltpu.VMEM(attn_shape, BF16),
            pltpu.VMEM((n, n_vec, rows), F32),
            pltpu.VMEM((n_vec, rows), F32),
            pltpu.VMEM((SEQ, n_vec, rows), F32),
        ]
    ] + [op.scratch for op in (attn_op, vec_sum, vec_op, main, attn_sum, wide_op)]
    groups.append(RowSum.scratch(count, (span, width)))
    late = (attn_moment, x_part, first_grad)
    groups.append([pltpu.VMEM(a.shape, a.dtype) for a in late] + [pltpu.SemaphoreType.DMA((3,))])

    def kernel(
        grad_attn, wide_in, bias_sums, vec_grad, attn_moment, wide_bf, x_part, first_grad,
        attn_all, wide_all, vec_total, input_grad, attn_orth, wide_orth, *rest,
    ):
        greet_signal(n, {"all"})
        parts, i = [], 0
        for group in groups:
            parts.append(rest[i : i + len(group)])
            i += len(group)
        attn_piece, attn_bf, attn_send, vec_local, vec_piece, vec_parts = parts[0]
        s = lax.axis_index("seq")
        arriving = [
            pltpu.make_async_copy(a, b, parts[8][3].at[k])
            for k, (a, b) in enumerate(zip((attn_moment, x_part, first_grad), parts[8][:3]))
        ]
        attn_moment, x_part, first_grad = parts[8][:3]
        for c in arriving:
            c.start()
        main_move = main.run(attn_send, wide_in, attn_orth, wide_orth, *parts[4])
        step(main_move)
        main.prepare()
        greet_wait(n, {"all"})
        x_sum = RowSum(x_part, *parts[7])

        def inputs():
            arriving[1].wait()
            arriving[2].wait()
            for r in range(count):
                x_sum.send_diag(r)
                x_sum.send_near(r)
            yield
            for r in range(count):
                x_sum.cross(r)
            yield from rounds(8)
            for r in range(count):
                input_grad[r] = x_sum.total(r) + first_grad[r]
                x_sum.finish(r)

        def attention():
            moving = attn_sum.run(grad_attn, attn_piece, *parts[5])
            step(moving)
            yield from rounds(3)
            for _ in range(n // 2 - 1):
                step(moving)
            yield from rounds(3)
            drain(moving)
            arriving[0].wait()
            for j in range(4):
                attn_bf[j] = fold(attn_piece[:, j * quarter : (j + 1) * quarter]).astype(BF16)
            for k in range(SEQ):

                @pl.when(s == k)
                def _(k=k):
                    for j in range(4):
                        old = fold(attn_moment[j, :, k * quarter : (k + 1) * quarter])
                        attn_send[j] = (matrix_decay * old + attn_bf[j].astype(F32)).astype(BF16)
            main.send_attn()
            yield
            main.attn_turn()
            yield from spaced(attn_op.run(attn_bf, attn_all, *parts[1]), 2)

        def vectors():
            def here(k, value):
                return jnp.where(s == k, value, 0.0)

            lines = [
                jnp.concatenate(
                    [here(k, bias_sums[:, j * quarter : (j + 1) * quarter]) for k in range(SEQ)], axis=1
                )
                for j in (0, 2)
            ]
            lines += [vec_grad[j : j + 1] for j in range(6)]
            hidden = vec_grad[6:7]
            pieces = [
                here(k, hidden[:, b * hid_own : (b + 1) * hid_own]) for b in range(n) for k in range(SEQ)
            ]
            each = n * SEQ // 4
            lines += [jnp.concatenate(pieces[j * each : (j + 1) * each], axis=1) for j in range(4)]
            whole = jnp.concatenate(lines, axis=0)
            for b in range(n):
                vec_local[b] = whole[:, b * rows : (b + 1) * rows]
            yield from spaced(vec_sum.run(vec_local, vec_piece, *parts[2]), 3)
            yield from spaced(vec_op.run(vec_piece, vec_parts, *parts[3]), 2)
            vec_total[...] = (vec_parts[0] + vec_parts[1]) + (vec_parts[2] + vec_parts[3])

        run_together(
            vectors(),
            attention(),
            inputs(),
            spaced(wide_op.run(wide_bf, wide_all, *parts[6]), 6),
            main_move,
        )

    vmem = pl.BlockSpec(memory_space=pltpu.VMEM)
    far = pl.BlockSpec(memory_space=pl.ANY)
    ins = (grad_attn, wide_in, bias_sums, vec_grad, attn_moment, wide_bf, x_part, first_grad)
    return pl.pallas_call(
        kernel,
        out_shape=outs,
        in_specs=[vmem, far, vmem, vmem, far, vmem, far, far],
        out_specs=[vmem] * len(outs),
        scratch_shapes=[c for group in groups for c in group],
        compiler_params=pltpu.CompilerParams(
            collective_id=8, has_side_effects=True, vmem_limit_bytes=62 * 2**20
        ),
        name="muon",
    )(*ins)


def finish(
    n, out_rows, pool_sum, input_grad, attn_all, wide_all, attn_orth, wide_orth, vec_total,
    attn_weight, up_weight, down_weight, vectors, attn_moment, up_moment, down_moment, vector_moment,
    factors, vector_step,
):
    rows = wide_all.shape[2]
    quarter = wide_all.shape[3] // SEQ
    shape = jax.ShapeDtypeStruct
    ins = (
        attn_all, attn_moment, wide_all, up_moment, down_moment, out_rows, input_grad, pool_sum, vec_total,
        vectors, vector_moment, attn_orth, attn_weight, wide_orth, up_weight, down_weight,
    )
    token, pool = shape(out_rows.shape, F32), shape((out_rows.shape[0], quarter), F32)
    attn, up, down, vec = [shape(a.shape, F32) for a in (attn_weight, up_weight, down_weight, vectors)]
    outs = [token, pool, token] + [attn, up, down, vec] * 3
    direct = {0: 5, 2: 6}
    held = [k for k in range(len(outs)) if k not in direct]

    def kernel(*refs):
        far_in, far_out = refs[: len(ins)], refs[len(ins) : len(ins) + len(outs)]
        refs = refs[len(ins) + len(outs) :]
        near_in = refs[: len(ins)]
        near_out = dict(zip(held, refs[len(ins) :]))
        near_out.update({k: near_in[j] for k, j in direct.items()})
        in_sem, out_sem = refs[-2:]
        arriving = [
            pltpu.make_async_copy(a, b, in_sem.at[k]) for k, (a, b) in enumerate(zip(far_in, near_in))
        ]
        leaving = [
            pltpu.make_async_copy(near_out[k], far_out[k], out_sem.at[k]) for k in range(len(outs))
        ]
        for c in arriving:
            c.start()
        (
            attn_all, attn_moment, wide_all, up_moment, down_moment, _, _, pool_sum, vec_total,
            vectors, vector_moment, attn_orth, attn_weight, wide_orth, up_weight, down_weight,
        ) = near_in
        (
            _, pooled, _, attn_grad, up_grad, down_grad, vec_grad, attn_next, up_next, down_next, vec_next,
            attn_new, up_new, down_new, vec_new,
        ) = [near_out[k] for k in range(len(outs))]

        def wait(*ks):
            for k in ks:
                arriving[k].wait()

        def leave(*ks):
            for k in ks:
                leaving[k].start()

        def attn_of(parts, j):
            return jnp.concatenate([unfold(parts[k, j]) for k in range(SEQ)], axis=1).astype(F32)

        wait(0, 1)
        for j in range(4):
            grad = attn_of(attn_all, j)
            attn_grad[j] = grad
            attn_next[j] = matrix_decay * attn_moment[j] + grad
        leave(3, 7)
        wait(2, 3)
        grad = join_up_parts([wide_all[k, 0] for k in range(SEQ)], n).astype(F32)
        up_grad[...] = grad
        up_next[...] = matrix_decay * up_moment[...] + grad
        leave(4, 8)
        wait(4)
        for k in range(SEQ):
            part = pl.ds(k * rows, rows)
            grad = wide_all[k, 1].astype(F32)
            down_grad[part] = grad
            down_next[part] = matrix_decay * down_moment[part] + grad
        leave(5, 9)
        wait(5)
        leave(0)
        wait(6)
        leave(2)
        wait(7, 8, 9, 10)
        s = lax.axis_index("seq")
        pooled[...] = sum(
            jnp.where(s == k, pool_sum[:, k * quarter : (k + 1) * quarter], 0.0) for k in range(SEQ)
        )
        vec_grad[...] = vec_total[...]
        moved = vector_decay * vector_moment[...] + vec_total[...]
        vec_next[...] = moved
        vec_new[...] = vectors[...] - vector_step * moved
        leave(1, 6, 10, 14)
        wait(11, 12)
        for j in range(4):
            attn_new[j] = attn_weight[j] - factors[0] * attn_of(attn_orth, j)
        leave(11)
        wait(13, 14)
        orth = join_up_parts([wide_orth[k, 0] for k in range(SEQ)], n).astype(F32)
        up_new[...] = up_weight[...] - factors[1] * orth
        leave(12)
        wait(15)
        for k in range(SEQ):
            part = pl.ds(k * rows, rows)
            down_new[part] = down_weight[part] - factors[2] * wide_orth[k, 1].astype(F32)
        leave(13)
        for c in leaving:
            c.wait()

    anywhere = pl.BlockSpec(memory_space=pl.ANY)
    return pl.pallas_call(
        kernel,
        out_shape=outs,
        in_specs=[anywhere] * len(ins),
        out_specs=[anywhere] * len(outs),
        scratch_shapes=[pltpu.VMEM(a.shape, a.dtype) for a in ins]
        + [pltpu.VMEM(outs[k].shape, F32) for k in held]
        + [pltpu.SemaphoreType.DMA((len(ins),)), pltpu.SemaphoreType.DMA((len(outs),))],
        compiler_params=pltpu.CompilerParams(vmem_limit_bytes=60 * 2**20),
        name="finish",
    )(*ins)


def step_factor(rows_all, cols_all):
    return matrix_rate * math.sqrt(max(1.0, rows_all / cols_all))


def make_body(n):
    def body(
        layer_input,
        lengths,
        attn_weight,
        up_weight,
        down_weight,
        vectors,
        attn_moment,
        up_moment,
        down_moment,
        vector_moment,
        out_grad,
        pool_grad,
    ):
        rows, span, width = layer_input.shape
        own_rows = width // n
        quarter = width // SEQ
        hidden = up_weight.shape[1]
        hid_q = hidden // SEQ
        hid_own = hidden // n // SEQ
        seq_index = lax.axis_index("seq")

        def attn_quarter(stacked):
            part = lax.dynamic_index_in_dim(
                stacked.reshape(4, own_rows, SEQ, quarter), seq_index, 2, False
            )
            return part

        def up_quarter(matrix):
            return lax.dynamic_index_in_dim(
                matrix.reshape(own_rows, n, SEQ, hid_own), seq_index, 2, False
            ).reshape(own_rows, hid_q)

        def down_quarter(matrix):
            return lax.dynamic_index_in_dim(
                matrix.reshape(SEQ, hid_own, width), seq_index, 0, False
            )

        aligned = own_rows % 16 == 0
        if aligned:
            own = [attn_weight, up_weight, down_weight]
            vec_own = vectors
        else:
            attn_low = attn_quarter(attn_weight).astype(BF16).transpose(1, 0, 2).reshape(own_rows, width)
            up_low = up_quarter(up_weight).astype(BF16)
            down_low = down_quarter(down_weight).astype(BF16)
            vec_low = vectors.astype(BF16).astype(F32)
            placed = lax.dynamic_update_slice(
                jnp.zeros((vectors.shape[0], n, own_rows), F32),
                vec_low[:, None],
                (0, lax.axis_index("batch"), 0),
            ).reshape(-1, width)
            bias_up = lax.dynamic_index_in_dim(
                placed[8:].reshape(n, SEQ, hid_own), seq_index, 1, False
            ).reshape(1, hid_q)
            bias_qv = lax.dynamic_index_in_dim(
                placed[:2].reshape(2, SEQ, quarter), seq_index, 1, False
            )
            blank = jnp.zeros((quarter,), F32)
            bias_qkv = jnp.concatenate([bias_qv[0], blank, bias_qv[1], blank])[None]
            vec_own = jnp.concatenate([placed[2:8], bias_up, bias_qkv])
            own = exchange(
                n, 1, "gather_weights", *[GatherBatch(n, a) for a in (attn_low, up_low, down_low)]
            )
            own = [a.reshape(width, width) for a in own]
        out_rows, pool_sum, input_grad, vec_grad, bias_sums, x_part, *grads = layer(
            n, layer_input, *own, vec_own, pool_grad, lengths, out_grad, up_moment, down_moment
        )
        factors = [
            step_factor(width, width),
            step_factor(width, hidden),
            step_factor(hidden, width),
        ]
        vector_step = vector_rate / math.sqrt(rows * n)
        if aligned:
            grad_attn, wide_bf, wide_in = grads
            attn_all, wide_all, vec_total, input_grad, attn_orth, wide_orth = muon(
                n, grad_attn, wide_in, bias_sums, vec_grad, attn_moment, wide_bf, x_part, input_grad
            )
            return tuple(
                finish(
                    n, out_rows, pool_sum, input_grad, attn_all, wide_all, attn_orth, wide_orth, vec_total,
                    attn_weight, up_weight, down_weight, vectors,
                    attn_moment, up_moment, down_moment, vector_moment, factors, vector_step,
                )
            )
        pooled = lax.dynamic_slice_in_dim(pool_sum, seq_index * quarter, quarter, 1)
        attn_piece, up_piece, down_piece = exchange(
            n, 2, "sum_grads", *[BatchSum(n, a.reshape(n, own_rows, width)) for a in grads]
        )
        bias_sums = bias_sums.reshape(3, quarter)

        vec_head = jnp.zeros((2, SEQ, quarter), F32)
        vec_head = lax.dynamic_update_slice(
            vec_head, bias_sums[jnp.array([0, 2])][:, None], (0, seq_index, 0)
        ).reshape(2, width)
        vec_mid = vec_grad[:6]
        grad_bias_up = vec_grad[6]
        vec_tail = lax.dynamic_update_slice(
            jnp.zeros((n, SEQ, hid_own), F32),
            grad_bias_up.reshape(n, 1, hid_own),
            (0, seq_index, 0),
        ).reshape(-1, width)
        vec_local = jnp.concatenate([vec_head, vec_mid, vec_tail])
        vec_local = vec_local.reshape(-1, n, own_rows).transpose(1, 0, 2)
        (vec_piece,) = exchange(n, 7, "sum_vectors", ScatterBatch(n, vec_local, F32))
        attn_bf = attn_piece.astype(BF16).reshape(own_rows, 4, quarter).transpose(1, 0, 2)
        wide_bf = jnp.stack([up_piece, down_piece]).astype(BF16)
        attn_send = (matrix_decay * attn_quarter(attn_moment) + attn_bf.astype(F32)).astype(BF16)
        wide_moment = jnp.stack([up_quarter(up_moment), down_quarter(down_moment)])
        wide_send = (matrix_decay * wide_moment + wide_bf.astype(F32)).astype(BF16)
        short = -own_rows % 16
        attn_send = jnp.pad(attn_send, ((0, 0), (0, short), (0, 0)))
        wide_send = jnp.pad(wide_send, ((0, 0), (0, short), (0, 0)))
        attn_all, wide_all, vec_parts, attn_orth, wide_orth = exchange(
            n,
            8,
            "muon",
            GatherSeq(n, attn_bf),
            GatherSeq(n, wide_bf),
            GatherSeq(n, vec_piece),
            Muon(n, attn_send, wide_send),
        )
        attn_orth = attn_orth[:, :, :own_rows]
        wide_orth = wide_orth[:, :, :own_rows]

        def join_attn(parts):
            return parts.astype(F32).transpose(1, 2, 0, 3).reshape(4, own_rows, width)

        def join_up(parts):
            return (
                parts.astype(F32)
                .reshape(SEQ, own_rows, n, hid_own)
                .transpose(1, 2, 0, 3)
                .reshape(own_rows, hidden)
            )

        def join_down(parts):
            return parts.astype(F32).reshape(SEQ * hid_own, width)

        attn_grad = join_attn(attn_all)
        up_grad, down_grad = join_up(wide_all[:, 0]), join_down(wide_all[:, 1])
        vector_grad = (vec_parts[0] + vec_parts[1]) + (vec_parts[2] + vec_parts[3])
        attn_next = matrix_decay * attn_moment + attn_grad
        up_next = matrix_decay * up_moment + up_grad
        down_next = matrix_decay * down_moment + down_grad

        attn_new = attn_weight - factors[0] * join_attn(attn_orth)
        up_new = up_weight - factors[1] * join_up(wide_orth[:, 0])
        down_new = down_weight - factors[2] * join_down(wide_orth[:, 1])
        vector_next = vector_decay * vector_moment + vector_grad
        vectors_new = vectors - vector_step * vector_next
        return (
            out_rows,
            pooled,
            input_grad,
            attn_grad,
            up_grad,
            down_grad,
            vector_grad,
            attn_next,
            up_next,
            down_next,
            vector_next,
            attn_new,
            up_new,
            down_new,
            vectors_new,
        )

    return body


def solution(mesh):
    placed = (
        P("batch", "seq", None),
        P("batch"),
        P(None, "batch", None),
        P("batch", None),
        P("batch", None),
        P(None, "batch"),
        P(None, "batch", None),
        P("batch", None),
        P("batch", None),
        P(None, "batch"),
        P("batch", "seq", None),
        P("batch", "seq"),
    )
    return jax.shard_map(
        make_body(mesh.shape["batch"]),
        mesh=mesh,
        in_specs=placed,
        out_specs=(
            P("batch", "seq", None),
            P("batch", "seq"),
            P("batch", "seq", None),
            P(None, "batch", None),
            P("batch", None),
            P("batch", None),
            P(None, "batch"),
            P(None, "batch", None),
            P("batch", None),
            P("batch", None),
            P(None, "batch"),
            P(None, "batch", None),
            P("batch", None),
            P("batch", None),
            P(None, "batch"),
        ),
        check_vma=False,
    )
```

profile of v0, /device:TPU:31, one launch (start us, length us, event | category | flops | bytes accessed | tf_op | source)
XLA Modules:
  0.0 223.9 jit_solution(4466345395590636973)
XLA Ops:
  0.6 126.8 %layer.1 = (f32[2,128,768]{2,1,0:T(8,128)}, f32[2,768]{1,0:T(2,128)}, f32[2,128,768]{2,1,0:T(8,128)}, f32[8,768]{1,0:T(8,128)}, f32[1,576]{1,0:T(1,128)}, /*inde...) custom-call(f32[2,128,768]{2,1,0:T(8,128)} %tokens.1, ...), custom_call_target="tpu_custom_call" | custom-call | tf_op jit(solution)/shard_map/layer/pallas_call | solution.py:1662
  127.4 86.6 %muon.1 = (bf16[4,4,48,384]{3,2,1,0:T(8,128)(2,1)}, bf16[4,2,96,768]{3,2,1,0:T(8,128)(2,1)}, f32[12,96]{1,0:T(8,128)}, f32[2,128,768]{2,1,0:T(8,128)}, bf16[4,4,...) custom-call(bf16[8,96,768]{2,1,0:T(8,128)(2,1)} %get-tuple-element.30.grad_attn, ...), custom_call_target="tpu_custom_call" | custom-call | tf_op jit(solution)/shard_map/muon/pallas_call | solution.py:1819
  214.0 9.6 %finish.1 = (f32[2,128,768]{2,1,0:T(8,128)}, f32[2,192]{1,0:T(2,128)}, f32[2,128,768]{2,1,0:T(8,128)}, f32[4,96,768]{2,1,0:T(8,128)}, f32[96,3072]{1,0:T(8,128)}...) custom-call(bf16[4,4,48,384]{3,2,1,0:T(8,128)(2,1)} %get-tuple-eleme, ...), custom_call_target="tpu_custom_call" | custom-call | tf_op jit(solution)/shard_map/finish/pallas_call | solution.py:1934
where the time goes:
time: 227 us; the launch traced here: 224 us
  Pallas kernels  223 us (98%)
    pallas_call x1, Pallas kernels, layer(): pl.pallas_call(kernel, out_shape=outs, in_specs=[vmem] + [far_spec] * 3 +...  127 us
    pallas_call x1, Pallas kernels, muon(): pl.pallas_call(kernel, out_shape=outs, in_specs=[vmem, far, vmem, vmem, f...  86.6 us
    pallas_call x1, Pallas kernels, finish(): pl.pallas_call(kernel, out_shape=outs, in_specs=[anywhere] * len(ins), ou...  9.64 us

commit v1 on v0

--- a/solution.py
+++ b/solution.py
@@ -1995,7 +1995,7 @@
             attn_low = attn_quarter(attn_weight).astype(BF16).transpose(1, 0, 2).reshape(own_rows, width)
             up_low = up_quarter(up_weight).astype(BF16)
             down_low = down_quarter(down_weight).astype(BF16)
-            vec_low = vectors.astype(BF16).astype(F32)
+            vec_low = lax.reduce_precision(vectors, 8, 7)
             placed = lax.dynamic_update_slice(
                 jnp.zeros((vectors.shape[0], n, own_rows), F32),
                 vec_low[:, None],

time: 227 us -> 227 us (level)
  no operation moved by 1% of the time
where the time goes in v1:
time: 227 us; the launch traced here: 224 us
  Pallas kernels  223 us (98%)
    pallas_call x1, Pallas kernels, layer(): pl.pallas_call(kernel, out_shape=outs, in_specs=[vmem] + [far_spec] * 3 +...  127 us
    pallas_call x1, Pallas kernels, muon(): pl.pallas_call(kernel, out_shape=outs, in_specs=[vmem, far, vmem, vmem, f...  86.6 us
    pallas_call x1, Pallas kernels, finish(): pl.pallas_call(kernel, out_shape=outs, in_specs=[anywhere] * len(ins), ou...  9.64 us

profile of v1, /device:TPU:31, one launch (start us, length us, event | category | flops | bytes accessed | tf_op | source)
XLA Modules:
  0.0 223.9 jit_solution(4466345395590636973)
XLA Ops:
  0.6 126.8 %layer.1 = (f32[2,128,768]{2,1,0:T(8,128)}, f32[2,768]{1,0:T(2,128)}, f32[2,128,768]{2,1,0:T(8,128)}, f32[8,768]{1,0:T(8,128)}, f32[1,576]{1,0:T(1,128)}, /*inde...) custom-call(f32[2,128,768]{2,1,0:T(8,128)} %tokens.1, ...), custom_call_target="tpu_custom_call" | custom-call | tf_op jit(solution)/shard_map/layer/pallas_call | solution.py:1662
  127.4 86.6 %muon.1 = (bf16[4,4,48,384]{3,2,1,0:T(8,128)(2,1)}, bf16[4,2,96,768]{3,2,1,0:T(8,128)(2,1)}, f32[12,96]{1,0:T(8,128)}, f32[2,128,768]{2,1,0:T(8,128)}, bf16[4,4,...) custom-call(bf16[8,96,768]{2,1,0:T(8,128)(2,1)} %get-tuple-element.30.grad_attn, ...), custom_call_target="tpu_custom_call" | custom-call | tf_op jit(solution)/shard_map/muon/pallas_call | solution.py:1819
  214.0 9.6 %finish.1 = (f32[2,128,768]{2,1,0:T(8,128)}, f32[2,192]{1,0:T(2,128)}, f32[2,128,768]{2,1,0:T(8,128)}, f32[4,96,768]{2,1,0:T(8,128)}, f32[96,3072]{1,0:T(8,128)}...) custom-call(bf16[4,4,48,384]{3,2,1,0:T(8,128)(2,1)} %get-tuple-eleme, ...), custom_call_target="tpu_custom_call" | custom-call | tf_op jit(solution)/shard_map/finish/pallas_call | solution.py:1934
